TPU v7x, 256 devices: a whole 4x4x8 slice. The times are simulated.
256 devices in a mesh: row: 16 (over z, core), col: 16 (over x, y).
Axes of the slice: x: 4, y: 4, z: 8, core: 2. Of those that a mesh axis runs over, the one named last changes fastest.
Arguments:
- student: bfloat16 [14336, 1024], P(('row', 'col')), may hold values from -0.5 to 0.5
- teacher: bfloat16 [14336, 4096], P(('row', 'col')), may hold values from -0.125 to 0.125
- scales: float32 [14336], P(('row', 'col')), may hold values from 0.3 to 3
Outputs:
- student_grad: float32 [14336, 1024], P(('row', 'col'))
All inputs are finite; a program needn't handle non-finite values.
Results may differ from a plain program's by a relative error of at most 0.004.
Values may be sent and summed in bfloat16 or wider, within the bound.
A program may use at most 64 MiB of HBM per device.

v0:
```python
import jax
import jax.numpy as jnp
from jax import lax
from jax.sharding import PartitionSpec as P


def inner_rows(left, right):
    return lax.dot_general(
        left, right, (((1,), (1,)), ((), ())), preferred_element_type=jnp.float32
    )


def per_device(student, teacher, scales):
    row_student, row_teacher, row_scales = (
        lax.all_gather(student, "col", axis=0, tiled=True),
        lax.all_gather(teacher, "col", axis=0, tiled=True),
        lax.all_gather(scales.astype(jnp.bfloat16), "col", axis=0, tiled=True).astype(scales.dtype),
    )
    col_student, col_teacher, col_scales = (
        lax.all_gather(student, "row", axis=0, tiled=True),
        lax.all_gather(teacher, "row", axis=0, tiled=True),
        lax.all_gather(scales.astype(jnp.bfloat16), "row", axis=0, tiled=True).astype(scales.dtype),
    )
    student_gram = inner_rows(row_student, col_student)
    teacher_gram = inner_rows(row_teacher, col_teacher) * row_scales[:, None] * col_scales[None, :]
    difference = jnp.clip(student_gram - teacher_gram, -0.25, 0.25).astype(jnp.bfloat16)
    own_rows = student.shape[0]
    all_texts = own_rows * lax.axis_size("row") * lax.axis_size("col")
    norming = 1.0 / jnp.sqrt(jnp.float32(all_texts))
    factor = 4.0 * norming
    return lax.psum_scatter(
        factor * jnp.dot(difference, col_student, preferred_element_type=jnp.float32),
        "col",
        scatter_dimension=0,
        tiled=True,
    )


def solution(mesh):
    return jax.shard_map(
        per_device,
        mesh=mesh,
        in_specs=(P(("row", "col"), None), P(("row", "col"), None), P(("row", "col"))),
        out_specs=P(("row", "col"), None),
        check_vma=False,
    )
```

profile of v0, /device:TPU:6, one launch (start us, length us, event | category | flops | bytes accessed | tf_op | source)
XLA Modules:
  0.0 329.9 jit_solution(9276400942908644077)
XLA Ops:
  6.5 0.7 all-gather.5.cloned.1.call-update
  7.3 0.0 all-gather.7.cloned.1.call-start
  7.3 0.7 all-gather.7.cloned.1.call-update
  8.0 0.0 all-gather.9.cloned.1.call-start
  8.1 0.7 all-gather.9.cloned.1.call-update
  8.7 0.0 all-gather.11.cloned.1.call-start
  8.8 0.5 all-gather.11.cloned.1.call-update
  9.3 0.0 reduce-scatter.4.cloned.1.call-start
  9.4 1.3 dynamic-slice.1
  10.6 1.3 dynamic-slice
  13.3 0.7 convert_element_type.13
  13.9 0.2 dynamic-update-slice.1
  14.1 29.2 %all-reduce.1 = bf16[896]{0:T(1024)(128)(2,1)S(1)} all-reduce(bf16[896]{0:T(1024)(128)(2,1)S(1)} %dynamic-update-slice.1), channel_id=1, replica_groups=mesh['row'=16,'col'=16] {'row'}, use_global_device_ids=true, to_apply=%add.1 | all-reduce | flops 896 | bytes 3584
  43.4 0.2 dynamic-update-slice
  43.6 33.9 %all-reduce = bf16[896]{0:T(1024)(128)(2,1)S(1)} all-reduce(bf16[896]{0:T(1024)(128)(2,1)S(1)} %dynamic-update-slice), channel_id=1, replica_groups=mesh['row'=16,'col'=16] {'col'}, use_global_device_ids=true, to_apply=%add | all-reduce | flops 896 | bytes 3584
  77.5 0.0 all-gather.5.cloned.1.call-done
  77.6 25.5 %all-gather.7.cloned.1.call-done = bf16[896,1024]{1,0:T(8,128)(2,1)} async-done(((bf16[56,1024]{1,0:T(8,128)(2,1)}), bf16[896,1024]{1,0:T(8,128)(2,1)}) %all-gather.7.cloned.1.call-update) | async-done | bytes 1835024 | tf_op jit(solution)/shard_map/all_gather | solution.py:20
  103.1 5.9 %fusion.6 = f32[896,896]{1,0:T(8,128)} fusion(bf16[896,1024]{1,0:T(8,128)(2,1)} %all-gather.5.cloned.1.call-done, bf16[896,1024]{1,0:T(8,128)(2,1)} %all-gather.7.cloned.1.call-done), kind=kOutput, calls=%fused_computation.8 | convolution fusion | flops 1644167168 | bytes 6881280 | tf_op jit(solution)/shard_map/dot_general | solution.py:8
  109.0 66.2 %all-gather.9.cloned.1.call-done = bf16[896,4096]{1,0:T(8,128)(2,1)} async-done(((bf16[56,4096]{1,0:T(8,128)(2,1)}), bf16[896,4096]{1,0:T(8,128)(2,1)}) %all-gather.9.cloned.1.call-update) | async-done | bytes 7340048 | tf_op jit(solution)/shard_map/all_gather | solution.py:16
  175.2 52.4 %all-gather.11.cloned.1.call-done = bf16[896,4096]{1,0:T(8,128)(2,1)} async-done(((bf16[56,4096]{1,0:T(8,128)(2,1)}), bf16[896,4096]{1,0:T(8,128)(2,1)}) %all-gather.11.cloned.1.call-update) | async-done | bytes 7340048 | tf_op jit(solution)/shard_map/all_gather | solution.py:21
  227.6 0.0 copy-done
  227.6 15.9 %convolution_multiply_fusion = f32[896,1024]{1,0:T(8,128)} fusion(bf16[896,1024]{1,0:T(8,128)(2,1)S(1)} %copy-done, f32[896,896]{1,0:T(8,128)} %fusion.6, bf16[896,4096]{1,0:T(8,128)(2,1)} %all-gather.9.cloned.1.call-done, bf16[896,4096]{1,0:T(8,128)(2,1)} %all-gather.11.cloned.1.call-done, f32[896]{0:T(1024)S(1)} %convert_element_type.15, ...), kind=kOutput, calls=%fused_computation.1 | convolution fusion | flops 8225767424 | bytes 23403520 | tf_op jit(solution)/shard_map/dot_general | solution.py:32
  243.5 0.0 reduce-scatter.4.cloned.1.call-update
  243.6 79.8 %reduce-scatter.4.cloned.1.call-done = f32[56,1024]{1,0:T(8,128)} async-done(((f32[896,1024]{1,0:T(8,128)}), f32[56,1024]{1,0:T(8,128)}) %reduce-scatter.4.cloned.1.call-update) | async-done | bytes 229392
  (6 shorter events, 0.0 us)
Async XLA Ops:
  6.5 71.0 %all-gather.5.cloned.1.call-start = ((), (), s32[]{:S(2)}) async-start(), calls=%async_computation.1 | async-start | bytes 1949696 | tf_op jit(solution)/shard_map/all_gather | solution.py:15
  7.3 95.8 %all-gather.7.cloned.1.call-start = ((), (), s32[]{:S(2)}) async-start(), calls=%async_computation.2 | async-start | bytes 1949696 | tf_op jit(solution)/shard_map/all_gather | solution.py:20
  8.0 167.2 %all-gather.9.cloned.1.call-start = ((), (), s32[]{:S(2)}) async-start(), calls=%async_computation.3 | async-start | bytes 7798784 | tf_op jit(solution)/shard_map/all_gather | solution.py:16
  8.7 218.9 %all-gather.11.cloned.1.call-start = ((), (), s32[]{:S(2)}) async-start(), calls=%async_computation.4 | async-start | bytes 7798784 | tf_op jit(solution)/shard_map/all_gather | solution.py:21
  9.3 314.0 %reduce-scatter.4.cloned.1.call-start = ((), (), s32[]{:S(2)}) async-start(), calls=%async_computation.5 | async-start | bytes 3899392
  103.1 124.6 %copy-start = (bf16[896,1024]{1,0:T(8,128)(2,1)S(1)}, bf16[896,1024]{1,0:T(8,128)(2,1)}, u32[]{:S(2)}) copy-start(bf16[896,1024]{1,0:T(8,128)(2,1)} %all-gather.7.cloned.1.call-done) | copy-start | bytes 5505028
Sparse Core Ops, SparseCore 0:
  9.8 52.2 all-gather.4
  64.0 39.0 all-gather.6
  105.6 69.5 all-gather.8
  176.9 50.7 all-gather.10
  243.7 79.6 reduce-scatter.3
where the time goes:
time: 330 us
  waiting for transfers between devices  227 us (69%)
  blocking collectives  63.2 us (19%)
  matrix products  21.8 us (7%)
  between operations  14.5 us (4%)
    unnamed x6, waiting for transfers between devices  82.4 us
    all_gather x1, waiting for transfers between devices, per_device(): lax.all_gather(teacher, 'col', axis=0, tiled=True)  66.2 us
    unnamed x2, blocking collectives  63.2 us
    all_gather x1, waiting for transfers between devices, per_device(): lax.all_gather(teacher, 'row', axis=0, tiled=True)  52.4 us
    all_gather x1, waiting for transfers between devices, per_device(): lax.all_gather(student, 'row', axis=0, tiled=True)  25.5 us
    dot_general x1, matrix products, per_device(): jnp.dot(difference, col_student, preferred_element_type=jnp.float32)  15.9 us
  transfers between devices with their start and end apart: 5, of which 4 were waited for; matrix products, arithmetic and copies ran while one was open for 3% of the time, Pallas kernels for 0%

commit v1 on v0

v1 whole, which is shorter than its diff:
```python
import functools
import jax
import jax.numpy as jnp
from jax import lax
from jax.experimental import pallas as pl
from jax.experimental.pallas import tpu as pltpu
from jax.sharding import PartitionSpec as P

DS, DT, ROWS, EXT = 1024, 4096, 56, 128
TEXTS = 14336
WIDTH = DT + DS + EXT
PIECES = ((0, 1280), (1280, 2560), (2560, 3840), (3840, WIDTH))
T_PIECES = ((0, 1280), (1280, 2560), (2560, 3840), (3840, DT))
LINKS = ("X+", "X-", "Y+", "Y-", "Z+", "Z-", "S")
GROUP = 4 * ROWS
WI = 512
WJ = DS - WI
QI, HJ = WI // 4, WJ // 2
LAG = 3
BUDGET = 1.5
RLAG = 4


def moved(block, link):
    step = 1 if link[1] == "+" else -1
    if link[0] == "X":
        return ((block[0] - step) % 4, block[1])
    return (block[0], (block[1] - step) % 4)


def gather_xy():
    out = []

    def ring(axis, heads, p, q):
        for head in heads:
            for link, far, order in ((axis + "+", p, (p, q)), (axis + "-", q, (q, p))):
                near = moved(head, link)
                out.extend((link, head, piece, near) for piece in order)
                out.append((link, near, far, moved(near, link)))

    ring("X", [(0, 0)], 0, 1)
    ring("Y", [(d, 0) for d in (0, 1, 3, 2)], 0, 1)
    ring("Y", [(0, 0)], 2, 3)
    ring("X", [(0, d) for d in (0, 1, 3, 2)], 2, 3)
    return out


def slots_of(moves, feeds, links, lag):
    n = len(moves)
    users = [[j for j in range(n) if i in feeds[j]] for i in range(n)]

    @functools.cache
    def height(i):
        return 1 + max([height(j) for j in users[i]], default=0)

    slot, now = {}, 0
    while len(slot) < n:
        now += 1
        for link in links:
            ready = [
                i for i in range(n)
                if i not in slot and moves[i][0] == link
                and all(f in slot and slot[f] + lag <= now for f in feeds[i])
            ]
            if ready:
                best = min(ready, key=lambda i: (-height(i), -len(users[i]), i))
                slot[best] = now
    return slot


def plan_gather():
    moves = gather_xy()
    source = {(m[3], m[2]): i for i, m in enumerate(moves)}
    feeds = [[source[(m[1], m[2])]] if (m[1], m[2]) in source else [] for m in moves]
    slot = slots_of(moves, feeds, LINKS[:4], LAG)
    return moves, feeds, slot


MOVES, FEEDS, SLOT = plan_gather()
LAST = max(SLOT.values())
ARRIVE = {}
for _i, _m in enumerate(MOVES):
    ARRIVE.setdefault(_m[3], {})[_m[2]] = SLOT[_i]
ARRIVE[(0, 0)] = {p: 0 for p in range(4)}
I_ORDER = sorted((b for b in ARRIVE if b != (0, 0)), key=lambda b: (max(ARRIVE[b].values()), sum(ARRIVE[b].values()), b))
I_ORDER = I_ORDER + [(0, 0)]
I_INDEX = {b: i for i, b in enumerate(I_ORDER)}
J_ORDER = [(0, 0), (0, 1), (4, 0), (4, 1)]
for _d in (1, 2, 3):
    J_ORDER += [(_d, 0), (8 - _d, 0), (_d, 1), (8 - _d, 1)]
J_INDEX = {b: 15 + i for i, b in enumerate(J_ORDER)}
BLOCKS = 31

Z_MOVES = []
for _s in range(14):
    _d, _p = _s // 4, _s % 4
    Z_MOVES.append(("Z+", (8 - _d) % 8, _p, 7 - _d, _s + 1))
    Z_MOVES.append(("Z-", _d, (_p + 2) % 4, _d + 1, _s + 1))
J_ARRIVE = {b: {p: 0 for p in range(4)} for b in J_ORDER}
for _m in Z_MOVES:
    J_ARRIVE[(_m[3], 0)][_m[2]] = _m[4]
    J_ARRIVE[(_m[3], 1)][_m[2]] = _m[4] + 1


def plan_compute():
    i_at = [[max(ARRIVE[b][p] for b in I_ORDER[4 * g:4 * g + 4]) for p in range(4)] for g in range(4)]
    j_at = [[max(J_ARRIVE[b][p] for b in J_ORDER[4 * g:4 * g + 4]) for p in range(4)] for g in range(4)]
    left = {(i, j): [0, 1, 2, 3] for i in range(4) for j in range(4)}
    started = set()
    done = {i: 0 for i in range(4)}
    out = {}

    def runs(pieces):
        ranges = []
        for p in pieces:
            if ranges and ranges[-1][1] == T_PIECES[p][0]:
                ranges[-1][1] = T_PIECES[p][1]
            else:
                ranges.append(list(T_PIECES[p]))
        return ranges

    def finish(now, i, j):
        tasks = [("final", i, j, runs(left.pop((i, j))), (i, j) in started)]
        done[i] += 1
        if done[i] == 4:
            tasks.append(("grad", i))
        return tasks

    for now in range(1, LAST + 1):
        seen = now - LAG
        cost, tasks = 0.0, []
        for want in (4, 2, 1):
            for i, j in list(left):
                ready = [p for p in left[(i, j)] if max(i_at[i][p], j_at[j][p]) <= seen]
                if len(ready) == len(left[(i, j)]):
                    if want == 4 and cost < BUDGET:
                        cost += 0.15 + 0.14 * len(ready)
                        tasks += finish(now, i, j)
                    continue
                ready = [p for p in ready if p != 3]
                if want != 4 and len(ready) >= want and cost < BUDGET:
                    tasks.append(("acc", i, j, runs(ready), (i, j) in started))
                    started.add((i, j))
                    left[(i, j)] = [p for p in left[(i, j)] if p not in ready]
                    cost += 0.14 * len(ready)
        out[now] = tasks
    for stage in range(LAST - LAG + 1, LAST + 1):
        tasks = []
        for i, j in sorted(left):
            if max(max(i_at[i]), max(j_at[j])) <= stage:
                tasks += finish(stage, i, j)
        out["after", stage] = tasks
    assert not left
    return out


TASKS = plan_compute()


def plan_reduce():
    moves = []

    def ring(axis, heads, p, q):
        def at(head, d):
            return ((head[0] + d) % 4, head[1]) if axis == "X" else (head[0], (head[1] + d) % 4)
        for head in heads:
            plus, minus = axis + "+", axis + "-"
            moves.append((plus, at(head, 2), p, at(head, 1)))
            moves.append((minus, at(head, 2), q, at(head, 3)))
            for piece in (q, p):
                moves.append((plus, at(head, 1), piece, head))
            for piece in (p, q):
                moves.append((minus, at(head, 3), piece, head))

    ring("Y", [(d, 0) for d in (2, 1, 3, 0)], 0, 1)
    ring("X", [(0, 0)], 0, 1)
    ring("X", [(0, d) for d in (2, 1, 3, 0)], 2, 3)
    ring("Y", [(0, 0)], 2, 3)
    feeds = [[j for j, f in enumerate(moves) if f[3] == m[1] and f[2] == m[2]] for m in moves]
    slot = slots_of(moves, feeds, LINKS[:4], RLAG)
    return moves, feeds, slot


R_MOVES, R_FEEDS, R_SLOT = plan_reduce()
RZ_MOVES = []
for _d in (4, 3, 2, 1):
    RZ_MOVES.append(("Z+", _d, 0, _d - 1))
    RZ_MOVES.append(("Z-", (8 - _d) % 8, 1, (9 - _d) % 8))
    if _d < 4:
        RZ_MOVES.append(("Z+", _d, 1, _d - 1))
        RZ_MOVES.append(("Z-", (8 - _d) % 8, 0, (9 - _d) % 8))
RZ_FEEDS = [[j for j, f in enumerate(RZ_MOVES) if f[3] == m[1] and f[2] == m[2]] for m in RZ_MOVES]


def dot(a, b, dims):
    return lax.dot_general(a, b, ((dims[0], dims[1]), ((), ())), preferred_element_type=jnp.float32)


def kernel(student, teacher, scales, out, X, acc, D, GI, GJ, RI, RJ, RS, load_sem, send, recv):
    row, col = lax.axis_index("row"), lax.axis_index("col")
    z, c = row // 2, row % 2
    x, y = col // 4, col % 4
    peer = {
        "X+": (row, ((x + 1) % 4) * 4 + y), "X-": (row, ((x + 3) % 4) * 4 + y),
        "Y+": (row, x * 4 + (y + 1) % 4), "Y-": (row, x * 4 + (y + 3) % 4),
        "Z+": (((z + 1) % 8) * 2 + c, col), "Z-": (((z + 7) % 8) * 2 + c, col),
        "S": (z * 2 + 1 - c, col),
    }
    loads = [
        pltpu.make_async_copy(teacher, X.at[15, :, pl.ds(0, DT)], load_sem.at[0]),
        pltpu.make_async_copy(student, X.at[15, :, pl.ds(DT, DS)], load_sem.at[1]),
    ]
    for load in loads:
        load.start()
    barrier = pltpu.get_barrier_semaphore()
    for link in LINKS:
        pl.semaphore_signal(barrier, inc=1, device_id=peer[link], device_id_type=pl.DeviceIdType.MESH)
    here = lax.broadcasted_iota(jnp.int32, (ROWS, ROWS), 0) == lax.broadcasted_iota(jnp.int32, (ROWS, ROWS), 1)
    scale = jnp.sum(jnp.where(here, jnp.broadcast_to(scales[...], (ROWS, ROWS)), 0.0), axis=1, keepdims=True)
    high = scale.astype(jnp.bfloat16).astype(jnp.float32)
    mid = (scale - high).astype(jnp.bfloat16).astype(jnp.float32)
    low = scale - high - mid
    lane = lax.broadcasted_iota(jnp.int32, (ROWS, EXT), 1)
    terms = jnp.where(lane == 0, high, jnp.where(lane == 1, mid, jnp.where(lane == 2, low, 0.0)))
    X[15, :, DT + DS:] = terms.astype(jnp.bfloat16)
    for load in loads:
        load.wait()
    pl.semaphore_wait(barrier, len(LINKS))

    copies = []

    def push(link, src, dst):
        n = len(copies)
        copy = pltpu.make_async_remote_copy(
            src_ref=src, dst_ref=dst, send_sem=send.at[n], recv_sem=recv.at[n],
            device_id=peer[link], device_id_type=pl.DeviceIdType.MESH,
        )
        copy.start()
        copies.append(copy)
        return copy

    def part(index, piece):
        low_col, high_col = PIECES[piece]
        return X.at[index, :, pl.ds(low_col, high_col - low_col)]

    def i_rows(g, a, b):
        return X[4 * g:4 * g + 4, :, a:b].reshape(GROUP, b - a)

    def j_rows(g, a, b):
        return X[15 + 4 * g:19 + 4 * g, :, a:b].reshape(GROUP, b - a)

    grads = set()

    def run(task):
        kind, i = task[:2]
        if kind == "grad":
            total = None
            for j in range(4):
                term = dot(D[i, j, :, :GROUP], j_rows(j, DT, DT + WI), ((1,), (0,)))
                total = term if total is None else total + term
            GI[4 * i:4 * i + 4] = total.reshape(4, ROWS, WI)
            for j in range(4):
                term = dot(D[i, j, :, :GROUP], i_rows(i, DT + WI, DT + DS), ((0,), (0,))).reshape(4, ROWS, WJ)
                if grads:
                    GJ[4 * j:4 * j + 4] += term
                else:
                    GJ[4 * j:4 * j + 4] = term
            grads.add(i)
            return
        j, ranges, started = task[2:]
        total = acc[i, j, :, :GROUP] if started else None
        for a, b in ranges:
            term = dot(i_rows(i, a, b), j_rows(j, a, b), ((1,), (1,)))
            total = term if total is None else total + term
        if kind == "acc":
            acc[i, j, :, :GROUP] = total
            return
        own = jnp.sum(i_rows(i, DT + DS, WIDTH).astype(jnp.float32), axis=1, keepdims=True)
        ones = jnp.ones((8, EXT), jnp.bfloat16)
        other = dot(ones, j_rows(j, DT + DS, WIDTH), ((1,), (1,)))[0:1]
        student_gram = dot(i_rows(i, DT, DT + DS), j_rows(j, DT, DT + DS), ((1,), (1,)))
        d = jnp.clip(student_gram - total * own * other, -0.25, 0.25)
        D[i, j, :, :GROUP] = d.astype(jnp.bfloat16)

    arriving, forwards = {}, {}
    first = push("S", X.at[15], X.at[J_INDEX[(0, 1)]])

    def wait_slot(s):
        if s == 0:
            first.wait_recv()
        for copy in forwards.pop(s - 1, []):
            copy.wait_recv()
        for copy in arriving.pop(("xy", s), []):
            copy.wait_recv()
        for copy, m in arriving.pop(("z", s), []):
            copy.wait_recv()
            forwards.setdefault(s, []).append(
                push("S", part(J_INDEX[(m[3], 0)], m[2]), part(J_INDEX[(m[3], 1)], m[2]))
            )

    for now in range(1, LAST + 1):
        if now > LAG - 1:
            wait_slot(now - LAG)
        for i, m in enumerate(MOVES):
            if SLOT[i] == now:
                copy = push(m[0], part(I_INDEX[m[1]], m[2]), part(I_INDEX[m[3]], m[2]))
                arriving.setdefault(("xy", now), []).append(copy)
        for m in Z_MOVES:
            if m[4] == now:
                copy = push(m[0], part(J_INDEX[(m[1], 0)], m[2]), part(J_INDEX[(m[3], 0)], m[2]))
                arriving.setdefault(("z", now), []).append((copy, m))
        for task in TASKS[now]:
            run(task)
    for stage in range(LAST - LAG + 1, LAST + 1):
        wait_slot(stage)
        for task in TASKS["after", stage]:
            run(task)
    assert not arriving and not forwards

    def cols(quarter):
        return pl.ds(quarter * QI, QI)

    def half(h):
        return pl.ds(h * HJ, HJ)

    shared = {}
    for d in (4, 3, 5, 2, 6, 1, 7, 0):
        shared[d] = push("S", GJ.at[J_INDEX[(d, 1)] - 15], RS.at[d])
    waiting = {}

    def collect(i):
        copy = waiting.pop(i)
        copy.wait_recv()
        m = R_MOVES[i]
        GI[I_INDEX[m[3]], :, cols(m[2])] += RI[i]

    def send_xy(i):
        m = R_MOVES[i]
        for f in R_FEEDS[i]:
            if f in waiting:
                collect(f)
        waiting[i] = push(m[0], GI.at[I_INDEX[m[1]], :, cols(m[2])], RI.at[i])

    z_waiting = {}

    def z_collect(i):
        copy = z_waiting.pop(i)
        copy.wait_recv()
        m = RZ_MOVES[i]
        GJ[J_INDEX[(m[3], 0)] - 15, :, half(m[2])] += RJ[i]

    def join(d):
        if d in shared:
            shared.pop(d).wait_recv()
            GJ[J_INDEX[(d, 0)] - 15] += RS[d]

    def send_z(i):
        m = RZ_MOVES[i]
        join(m[1])
        for f in RZ_FEEDS[i]:
            if f in z_waiting:
                z_collect(f)
        z_waiting[i] = push(m[0], GJ.at[J_INDEX[(m[1], 0)] - 15, :, half(m[2])], RJ.at[i])

    order = [(R_SLOT[i], 0, i) for i in range(len(R_MOVES))]
    z_slot = {"Z+": 1, "Z-": 1}
    for i, m in enumerate(RZ_MOVES):
        order.append((z_slot[m[0]], 1, i))
        z_slot[m[0]] += 2
    for _, kind, i in sorted(order):
        (send_z if kind else send_xy)(i)
    join(0)
    for i in sorted(waiting):
        collect(i)
    for i in sorted(z_waiting):
        z_collect(i)
    factor = 4.0 / jnp.sqrt(jnp.float32(TEXTS))
    out[:, :WI] = factor * GI[I_INDEX[(0, 0)]]
    out[:, WI:] = factor * GJ[0]
    for copy in copies:
        copy.wait_send()


COPIES = 1 + len(MOVES) + 2 * len(Z_MOVES) + 8 + len(R_MOVES) + len(RZ_MOVES)


def per_device(student, teacher, scales):
    return pl.pallas_call(
        kernel,
        out_shape=jax.ShapeDtypeStruct((ROWS, DS), jnp.float32),
        in_specs=[
            pl.BlockSpec(memory_space=pl.ANY),
            pl.BlockSpec(memory_space=pl.ANY),
            pl.BlockSpec(memory_space=pltpu.VMEM),
        ],
        out_specs=pl.BlockSpec(memory_space=pltpu.VMEM),
        scratch_shapes=[
            pltpu.VMEM((BLOCKS, ROWS, WIDTH), jnp.bfloat16),
            pltpu.VMEM((4, 4, GROUP, 256), jnp.float32),
            pltpu.VMEM((4, 4, GROUP, 256), jnp.bfloat16),
            pltpu.VMEM((16, ROWS, WI), jnp.float32),
            pltpu.VMEM((16, ROWS, WJ), jnp.float32),
            pltpu.VMEM((len(R_MOVES), ROWS, QI), jnp.float32),
            pltpu.VMEM((len(RZ_MOVES), ROWS, HJ), jnp.float32),
            pltpu.VMEM((8, ROWS, WJ), jnp.float32),
            pltpu.SemaphoreType.DMA((2,)),
            pltpu.SemaphoreType.DMA((COPIES,)),
            pltpu.SemaphoreType.DMA((COPIES,)),
        ],
        compiler_params=pltpu.CompilerParams(
            collective_id=0, has_side_effects=True, vmem_limit_bytes=56 * 2**20
        ),
        cost_estimate=pl.CostEstimate(flops=10**10, bytes_accessed=10**6, transcendentals=0),
        name="huber_gram",
    )(student, teacher, scales.reshape(1, ROWS))


def solution(mesh):
    return jax.shard_map(
        per_device,
        mesh=mesh,
        in_specs=(P(("row", "col"), None), P(("row", "col"), None), P(("row", "col"))),
        out_specs=P(("row", "col"), None),
        check_vma=False,
    )
```

time: 330 us -> 90.1 us (0.27)
  waiting for transfers between devices: 227 us -> 0 us
  Pallas kernels: 0 us -> 87.7 us
  blocking collectives: 63.2 us -> 0 us
  matrix products: 21.8 us -> 0 us
  between operations: 14.5 us -> 0.01 us
    all_gather x4 -> x0, waiting for transfers between devices: 144 us -> none  [the longest x1 66.2 us: per_device(): lax.all_gather(teacher, 'col', axis=0, tiled=True)]
    pallas_call x0 -> x1, Pallas kernels: none -> 87.7 us  [per_device(): pl.pallas_call(kernel, out_shape=jax.ShapeDtypeStruct((ROWS, DS), jnp.flo...]
    unnamed x6 -> x0, waiting for transfers between devices: 82.4 us -> none
    unnamed x2 -> x0, blocking collectives: 63.2 us -> none
    dot_general x2 -> x0, matrix products: 21.8 us -> none  [the longest x1 15.9 us: per_device(): jnp.dot(difference, col_student, preferred_element_type=jnp.float32)]
  transfers between devices with their start and end apart: 5 -> 0, of which waited for: 4 -> 0; matrix products, arithmetic and copies ran while one was open for 3% -> 0% of each run, Pallas kernels for 0% -> 0%
where the time goes in v1:
time: 90.1 us; the launch traced here: 89.4 us
  Pallas kernels  87.7 us (97%)
  local copies, waits for them, and re-layouts  1.64 us (2%)
    pallas_call x1, Pallas kernels, per_device(): pl.pallas_call(kernel, out_shape=jax.ShapeDtypeStruct((ROWS, DS), jnp.flo...  87.7 us

profile of v1, /device:TPU:6, one launch (start us, length us, event | category | flops | bytes accessed | tf_op | source)
XLA Modules:
  0.0 89.4 jit_solution(15446131716868675559)
XLA Ops:
  0.0 87.7 %huber_gram.1 = f32[56,1024]{1,0:T(8,128)} custom-call(bf16[56,1024]{1,0:T(8,128)(2,1)} %student.1, bf16[56,4096]{1,0:T(8,128)(2,1)} %teacher.1, f32[1,56]{1,0:T(1,128)} %bitcast.1), custom_call_target="tpu_custom_call" | custom-call | flops 10000000000 | bytes 1000000 | tf_op jit(solution)/shard_map/huber_gram/pallas_call | solution.py:388
  87.7 1.6 %copy.5 = f32[56,1024]{1,0:T(8,128)} copy(f32[56,1024]{1,0:T(8,128)} %huber_gram.1) | data formatting | bytes 458752

commit v2 on v1

--- a/solution.py
+++ b/solution.py
@@ -15,10 +15,11 @@
 GROUP = 4 * ROWS
 WI = 512
 WJ = DS - WI
-QI, HJ = WI // 4, WJ // 2
+QI, HJ = WI // 4, WJ // 4
 LAG = 3
-BUDGET = 1.5
-RLAG = 4
+BUDGET = 2.2
+HOP = 2.2
+S_HOP = 2.5
 
 
 def moved(block, link):
@@ -39,9 +40,9 @@
                 out.append((link, near, far, moved(near, link)))
 
     ring("X", [(0, 0)], 0, 1)
-    ring("Y", [(d, 0) for d in (0, 1, 3, 2)], 0, 1)
+    ring("Y", [(d, 0) for d in (2, 1, 3, 0)], 0, 1)
     ring("Y", [(0, 0)], 2, 3)
-    ring("X", [(0, d) for d in (0, 1, 3, 2)], 2, 3)
+    ring("X", [(0, d) for d in (2, 1, 3, 0)], 2, 3)
     return out
 
 
@@ -63,7 +64,7 @@
                 and all(f in slot and slot[f] + lag <= now for f in feeds[i])
             ]
             if ready:
-                best = min(ready, key=lambda i: (-height(i), -len(users[i]), i))
+                best = min(ready, key=lambda i: (-height(i), -len(users[i]), not {moves[i][3][0], moves[i][3][1]} & {2}, i))
                 slot[best] = now
     return slot
 
@@ -82,14 +83,14 @@
 for _i, _m in enumerate(MOVES):
     ARRIVE.setdefault(_m[3], {})[_m[2]] = SLOT[_i]
 ARRIVE[(0, 0)] = {p: 0 for p in range(4)}
-I_ORDER = sorted((b for b in ARRIVE if b != (0, 0)), key=lambda b: (max(ARRIVE[b].values()), sum(ARRIVE[b].values()), b))
-I_ORDER = I_ORDER + [(0, 0)]
+I_ORDER = sorted(ARRIVE, key=lambda b: (max(ARRIVE[b].values()), sum(ARRIVE[b].values()), b))
 I_INDEX = {b: i for i, b in enumerate(I_ORDER)}
 J_ORDER = [(0, 0), (0, 1), (4, 0), (4, 1)]
 for _d in (1, 2, 3):
     J_ORDER += [(_d, 0), (8 - _d, 0), (_d, 1), (8 - _d, 1)]
-J_INDEX = {b: 15 + i for i, b in enumerate(J_ORDER)}
-BLOCKS = 31
+J_INDEX = {b: 16 + i for i, b in enumerate(J_ORDER)}
+OWN, OWN_J = I_INDEX[(0, 0)], J_INDEX[(0, 0)]
+BLOCKS = 32
 
 Z_MOVES = []
 for _s in range(14):
@@ -102,6 +103,9 @@
     J_ARRIVE[(_m[3], 1)][_m[2]] = _m[4] + 1
 
 
+FIRST = {(0, 0), (1, 0), (2, 0)}
+
+
 def plan_compute():
     i_at = [[max(ARRIVE[b][p] for b in I_ORDER[4 * g:4 * g + 4]) for p in range(4)] for g in range(4)]
     j_at = [[max(J_ARRIVE[b][p] for b in J_ORDER[4 * g:4 * g + 4]) for p in range(4)] for g in range(4)]
@@ -119,38 +123,47 @@
                 ranges.append(list(T_PIECES[p]))
         return ranges
 
-    def finish(now, i, j):
-        tasks = [("final", i, j, runs(left.pop((i, j))), (i, j) in started)]
-        done[i] += 1
-        if done[i] == 4:
-            tasks.append(("grad", i))
-        return tasks
+    def pick(seen, budget, least, j_seen=None, only=None):
+        cost, tasks = 0.0, []
+        while cost < budget:
+            best = None
+            for i, j in sorted(left if only is None else only & set(left)):
+                ready = [p for p in left[(i, j)] if i_at[i][p] <= seen and j_at[j][p] <= (j_seen or seen)]
+                final = len(ready) == len(left[(i, j)])
+                ready = ready if final else [p for p in ready if p != 3]
+                if final or len(ready) >= least:
+                    key = (final, len(ready), -i)
+                    if best is None or key > best[0]:
+                        best = (key, i, j, ready, final)
+            if best is None:
+                break
+            _, i, j, ready, final = best
+            cost += 0.14 * len(ready) + (0.15 if final else 0.02)
+            tasks.append(("final" if final else "acc", i, j, runs(ready), (i, j) in started))
+            started.add((i, j))
+            left[(i, j)] = [p for p in left[(i, j)] if p not in ready]
+            if final:
+                del left[(i, j)]
+                done[i] += 1
+                if done[i] == 4:
+                    tasks.append(("grad", i))
+                    cost += 0.3
+        return tasks, cost
 
     for now in range(1, LAST + 1):
-        seen = now - LAG
-        cost, tasks = 0.0, []
-        for want in (4, 2, 1):
-            for i, j in list(left):
-                ready = [p for p in left[(i, j)] if max(i_at[i][p], j_at[j][p]) <= seen]
-                if len(ready) == len(left[(i, j)]):
-                    if want == 4 and cost < BUDGET:
-                        cost += 0.15 + 0.14 * len(ready)
-                        tasks += finish(now, i, j)
-                    continue
-                ready = [p for p in ready if p != 3]
-                if want != 4 and len(ready) >= want and cost < BUDGET:
-                    tasks.append(("acc", i, j, runs(ready), (i, j) in started))
-                    started.add((i, j))
-                    left[(i, j)] = [p for p in left[(i, j)] if p not in ready]
-                    cost += 0.14 * len(ready)
-        out[now] = tasks
-    for stage in range(LAST - LAG + 1, LAST + 1):
+        out[now], _ = pick(now - LAG, BUDGET, 1 if now > LAST - 5 else 2)
+    for stage in range(LAST - LAG + 1, LAST):
+        out["after", stage], _ = pick(stage, 9.0, 1, None, FIRST if stage == LAST - 1 else None)
+    out["after", LAST], _ = pick(LAST - 1, 9.0, 1, LAST, FIRST)
+    for j in (0, 3, 2, 1):
         tasks = []
-        for i, j in sorted(left):
-            if max(max(i_at[i]), max(j_at[j])) <= stage:
-                tasks += finish(stage, i, j)
-        out["after", stage] = tasks
+        for i in range(4):
+            if (i, j) in left:
+                tasks.append(("final", i, j, runs(left.pop((i, j))), (i, j) in started))
+                done[i] += 1
+        out["last", j] = tasks
     assert not left
+    out["late"] = [i for i in range(4) if ("grad", i) not in sum((v for v in out.values() if isinstance(v, list)), [])]
     return out
 
 
@@ -177,19 +190,44 @@
     ring("X", [(0, d) for d in (2, 1, 3, 0)], 2, 3)
     ring("Y", [(0, 0)], 2, 3)
     feeds = [[j for j, f in enumerate(moves) if f[3] == m[1] and f[2] == m[2]] for m in moves]
-    slot = slots_of(moves, feeds, LINKS[:4], RLAG)
-    return moves, feeds, slot
-
-
-R_MOVES, R_FEEDS, R_SLOT = plan_reduce()
+    return moves, feeds
+
+
+R_MOVES, R_FEEDS = plan_reduce()
 RZ_MOVES = []
 for _d in (4, 3, 2, 1):
-    RZ_MOVES.append(("Z+", _d, 0, _d - 1))
-    RZ_MOVES.append(("Z-", (8 - _d) % 8, 1, (9 - _d) % 8))
-    if _d < 4:
-        RZ_MOVES.append(("Z+", _d, 1, _d - 1))
-        RZ_MOVES.append(("Z-", (8 - _d) % 8, 0, (9 - _d) % 8))
+    for _q in (0, 1):
+        RZ_MOVES.append(("Z+", _d, _q, _d - 1))
+        RZ_MOVES.append(("Z-", (8 - _d) % 8, 2 + _q, (9 - _d) % 8))
+    for _q in (0, 1):
+        if _d < 4:
+            RZ_MOVES.append(("Z+", _d, 2 + _q, _d - 1))
+            RZ_MOVES.append(("Z-", (8 - _d) % 8, _q, (9 - _d) % 8))
 RZ_FEEDS = [[j for j, f in enumerate(RZ_MOVES) if f[3] == m[1] and f[2] == m[2]] for m in RZ_MOVES]
+
+
+def timed(moves, feeds, ready, length):
+    n = len(moves)
+    users = [[j for j in range(n) if i in feeds[j]] for i in range(n)]
+
+    @functools.cache
+    def height(i):
+        return 1 + max([height(j) for j in users[i]], default=0)
+
+    start, free = {}, {}
+    while len(start) < n:
+        best = None
+        for i in range(n):
+            if i in start or any(f not in start for f in feeds[i]):
+                continue
+            at = max([ready[i], free.get(moves[i][0], -9.0)] + [start[f] + length[i] + HOP for f in feeds[i]])
+            key = (at, -height(i), i)
+            if best is None or key < best:
+                best = key
+        at, _, i = best
+        start[i] = at
+        free[moves[i][0]] = at + length[i]
+    return start
 
 
 def dot(a, b, dims):
@@ -207,8 +245,10 @@
         "S": (z * 2 + 1 - c, col),
     }
     loads = [
-        pltpu.make_async_copy(teacher, X.at[15, :, pl.ds(0, DT)], load_sem.at[0]),
-        pltpu.make_async_copy(student, X.at[15, :, pl.ds(DT, DS)], load_sem.at[1]),
+        pltpu.make_async_copy(teacher, X.at[OWN, :, pl.ds(0, DT)], load_sem.at[0]),
+        pltpu.make_async_copy(student, X.at[OWN, :, pl.ds(DT, DS)], load_sem.at[1]),
+        pltpu.make_async_copy(teacher, X.at[OWN_J, :, pl.ds(0, DT)], load_sem.at[2]),
+        pltpu.make_async_copy(student, X.at[OWN_J, :, pl.ds(DT, DS)], load_sem.at[3]),
     ]
     for load in loads:
         load.start()
@@ -222,7 +262,8 @@
     low = scale - high - mid
     lane = lax.broadcasted_iota(jnp.int32, (ROWS, EXT), 1)
     terms = jnp.where(lane == 0, high, jnp.where(lane == 1, mid, jnp.where(lane == 2, low, 0.0)))
-    X[15, :, DT + DS:] = terms.astype(jnp.bfloat16)
+    X[OWN, :, DT + DS:] = terms.astype(jnp.bfloat16)
+    X[OWN_J, :, DT + DS:] = terms.astype(jnp.bfloat16)
     for load in loads:
         load.wait()
     pl.semaphore_wait(barrier, len(LINKS))
@@ -247,25 +288,28 @@
         return X[4 * g:4 * g + 4, :, a:b].reshape(GROUP, b - a)
 
     def j_rows(g, a, b):
-        return X[15 + 4 * g:19 + 4 * g, :, a:b].reshape(GROUP, b - a)
-
-    grads = set()
+        return X[16 + 4 * g:20 + 4 * g, :, a:b].reshape(GROUP, b - a)
+
+    def grad_i(i):
+        total = None
+        for j in range(4):
+            term = dot(D[i, j, :, :GROUP], j_rows(j, DT, DT + WI), ((1,), (0,)))
+            total = term if total is None else total + term
+        for q in range(4):
+            GI[q, 4 * i:4 * i + 4] = total[:, q * QI:(q + 1) * QI].reshape(4, ROWS, QI)
+
+    def grad_j(j):
+        total = None
+        for i in range(4):
+            term = dot(D[i, j, :, :GROUP], i_rows(i, DT + WI, DT + DS), ((0,), (0,)))
+            total = term if total is None else total + term
+        for h in range(4):
+            GJ[h, 4 * j:4 * j + 4] = total[:, h * HJ:(h + 1) * HJ].reshape(4, ROWS, HJ)
 
     def run(task):
         kind, i = task[:2]
         if kind == "grad":
-            total = None
-            for j in range(4):
-                term = dot(D[i, j, :, :GROUP], j_rows(j, DT, DT + WI), ((1,), (0,)))
-                total = term if total is None else total + term
-            GI[4 * i:4 * i + 4] = total.reshape(4, ROWS, WI)
-            for j in range(4):
-                term = dot(D[i, j, :, :GROUP], i_rows(i, DT + WI, DT + DS), ((0,), (0,))).reshape(4, ROWS, WJ)
-                if grads:
-                    GJ[4 * j:4 * j + 4] += term
-                else:
-                    GJ[4 * j:4 * j + 4] = term
-            grads.add(i)
+            grad_i(i)
             return
         j, ranges, started = task[2:]
         total = acc[i, j, :, :GROUP] if started else None
@@ -283,7 +327,7 @@
         D[i, j, :, :GROUP] = d.astype(jnp.bfloat16)
 
     arriving, forwards = {}, {}
-    first = push("S", X.at[15], X.at[J_INDEX[(0, 1)]])
+    first = push("S", X.at[OWN_J], X.at[J_INDEX[(0, 1)]])
 
     def wait_slot(s):
         if s == 0:
@@ -311,48 +355,49 @@
                 arriving.setdefault(("z", now), []).append((copy, m))
         for task in TASKS[now]:
             run(task)
-    for stage in range(LAST - LAG + 1, LAST + 1):
+    for stage in range(LAST - LAG + 1, LAST):
         wait_slot(stage)
         for task in TASKS["after", stage]:
             run(task)
-    assert not arriving and not forwards
-
-    def cols(quarter):
-        return pl.ds(quarter * QI, QI)
-
-    def half(h):
-        return pl.ds(h * HJ, HJ)
-
-    shared = {}
-    for d in (4, 3, 5, 2, 6, 1, 7, 0):
-        shared[d] = push("S", GJ.at[J_INDEX[(d, 1)] - 15], RS.at[d])
-    waiting = {}
+    for copy in forwards.pop(LAST - 1, []):
+        copy.wait_recv()
+    for task in TASKS["after", LAST]:
+        run(task)
+    shared, waiting, z_waiting = {}, {}, {}
+
+    def last(j):
+        for task in TASKS["last", j]:
+            run(task)
+        grad_j(j)
+        for d, core in reversed(J_ORDER[4 * j:4 * j + 4]):
+            if core == 1:
+                shared[d] = push("S", GJ.at[:, J_INDEX[(d, 1)] - 16], RS.at[d])
 
     def collect(i):
-        copy = waiting.pop(i)
-        copy.wait_recv()
+        if i not in waiting:
+            return
+        waiting.pop(i).wait_recv()
         m = R_MOVES[i]
-        GI[I_INDEX[m[3]], :, cols(m[2])] += RI[i]
+        GI[m[2], I_INDEX[m[3]]] += RI[i]
 
     def send_xy(i):
         m = R_MOVES[i]
         for f in R_FEEDS[i]:
             if f in waiting:
                 collect(f)
-        waiting[i] = push(m[0], GI.at[I_INDEX[m[1]], :, cols(m[2])], RI.at[i])
-
-    z_waiting = {}
+        waiting[i] = push(m[0], GI.at[m[2], I_INDEX[m[1]]], RI.at[i])
 
     def z_collect(i):
-        copy = z_waiting.pop(i)
-        copy.wait_recv()
+        if i not in z_waiting:
+            return
+        z_waiting.pop(i).wait_recv()
         m = RZ_MOVES[i]
-        GJ[J_INDEX[(m[3], 0)] - 15, :, half(m[2])] += RJ[i]
+        GJ[m[2], J_INDEX[(m[3], 0)] - 16] += RJ[i]
 
     def join(d):
         if d in shared:
             shared.pop(d).wait_recv()
-            GJ[J_INDEX[(d, 0)] - 15] += RS[d]
+            GJ[:, J_INDEX[(d, 0)] - 16] += RS[d]
 
     def send_z(i):
         m = RZ_MOVES[i]
@@ -360,23 +405,37 @@
         for f in RZ_FEEDS[i]:
             if f in z_waiting:
                 z_collect(f)
-        z_waiting[i] = push(m[0], GJ.at[J_INDEX[(m[1], 0)] - 15, :, half(m[2])], RJ.at[i])
-
-    order = [(R_SLOT[i], 0, i) for i in range(len(R_MOVES))]
-    z_slot = {"Z+": 1, "Z-": 1}
-    for i, m in enumerate(RZ_MOVES):
-        order.append((z_slot[m[0]], 1, i))
-        z_slot[m[0]] += 2
-    for _, kind, i in sorted(order):
-        (send_z if kind else send_xy)(i)
+        z_waiting[i] = push(m[0], GJ.at[m[2], J_INDEX[(m[1], 0)] - 16], RJ.at[i])
+
+    steps, clock, j_ready, i_ready = [(-0.1, 0, wait_slot, LAST)], 0.0, {}, [-1.0] * 4
+    for n, j in enumerate((0, 3, 2, 1)):
+        steps.append((clock, n, last, j))
+        clock += 0.3 + 0.75 * len(TASKS["last", j])
+        for d, core in J_ORDER[4 * j:4 * j + 4]:
+            j_ready[d] = clock + S_HOP
+    for i in TASKS["late"]:
+        steps.append((clock, 4 + i, grad_i, i))
+        clock += 0.3
+        i_ready[i] = clock
+    starts = timed(R_MOVES, R_FEEDS, [i_ready[I_INDEX[m[1]] // 4] for m in R_MOVES], [0.62] * len(R_MOVES))
+    for i, at in starts.items():
+        steps.append((at, 10 + i, send_xy, i))
+        got = max(at + 0.62 + HOP, i_ready[I_INDEX[R_MOVES[i][3]] // 4])
+        steps.append((got, 200 + i, collect, i))
+    starts = timed(RZ_MOVES, RZ_FEEDS, [j_ready[m[1]] for m in RZ_MOVES], [0.62] * len(RZ_MOVES))
+    for i, at in starts.items():
+        steps.append((at, 100 + i, send_z, i))
+        got = max(at + 0.62 + HOP, j_ready[RZ_MOVES[i][3]])
+        steps.append((got, 300 + i, z_collect, i))
+    for _, _, act, what in sorted(steps, key=lambda step: step[:2]):
+        act(what)
+    assert not arriving and not forwards
     join(0)
-    for i in sorted(waiting):
-        collect(i)
-    for i in sorted(z_waiting):
-        z_collect(i)
     factor = 4.0 / jnp.sqrt(jnp.float32(TEXTS))
-    out[:, :WI] = factor * GI[I_INDEX[(0, 0)]]
-    out[:, WI:] = factor * GJ[0]
+    for q in range(4):
+        out[:, q * QI:(q + 1) * QI] = factor * GI[q, I_INDEX[(0, 0)]]
+    for h in range(4):
+        out[:, WI + h * HJ:WI + (h + 1) * HJ] = factor * GJ[h, 0]
     for copy in copies:
         copy.wait_send()
 
@@ -398,12 +457,12 @@
             pltpu.VMEM((BLOCKS, ROWS, WIDTH), jnp.bfloat16),
             pltpu.VMEM((4, 4, GROUP, 256), jnp.float32),
             pltpu.VMEM((4, 4, GROUP, 256), jnp.bfloat16),
-            pltpu.VMEM((16, ROWS, WI), jnp.float32),
-            pltpu.VMEM((16, ROWS, WJ), jnp.float32),
+            pltpu.VMEM((4, 16, ROWS, QI), jnp.float32),
+            pltpu.VMEM((4, 16, ROWS, HJ), jnp.float32),
             pltpu.VMEM((len(R_MOVES), ROWS, QI), jnp.float32),
             pltpu.VMEM((len(RZ_MOVES), ROWS, HJ), jnp.float32),
-            pltpu.VMEM((8, ROWS, WJ), jnp.float32),
-            pltpu.SemaphoreType.DMA((2,)),
+            pltpu.VMEM((8, 4, ROWS, HJ), jnp.float32),
+            pltpu.SemaphoreType.DMA((4,)),
             pltpu.SemaphoreType.DMA((COPIES,)),
             pltpu.SemaphoreType.DMA((COPIES,)),
         ],

time: 90.1 us -> 87.2 us (0.968)
  Pallas kernels: 87.7 us -> 85.4 us
    pallas_call x1, Pallas kernels: 87.7 us -> 85.4 us  [per_device(): pl.pallas_call(kernel, out_shape=jax.ShapeDtypeStruct((ROWS, DS), jnp.flo...]
where the time goes in v2:
time: 87.2 us; the launch traced here: 87.1 us
  Pallas kernels  85.4 us (98%)
  local copies, waits for them, and re-layouts  1.64 us (2%)
    pallas_call x1, Pallas kernels, per_device(): pl.pallas_call(kernel, out_shape=jax.ShapeDtypeStruct((ROWS, DS), jnp.flo...  85.4 us

profile of v2, /device:TPU:6, one launch (start us, length us, event | category | flops | bytes accessed | tf_op | source)
XLA Modules:
  0.0 87.1 jit_solution(520581374381584477)
XLA Ops:
  0.0 85.4 %huber_gram.1 = f32[56,1024]{1,0:T(8,128)} custom-call(bf16[56,1024]{1,0:T(8,128)(2,1)} %student.1, bf16[56,4096]{1,0:T(8,128)(2,1)} %teacher.1, f32[1,56]{1,0:T(1,128)} %bitcast.1), custom_call_target="tpu_custom_call" | custom-call | flops 10000000000 | bytes 1000000 | tf_op jit(solution)/shard_map/huber_gram/pallas_call | solution.py:447
  85.4 1.6 %copy.5 = f32[56,1024]{1,0:T(8,128)} copy(f32[56,1024]{1,0:T(8,128)} %huber_gram.1) | data formatting | bytes 458752

commit v3 on v2

--- a/solution.py
+++ b/solution.py
@@ -6,9 +6,9 @@
 from jax.experimental.pallas import tpu as pltpu
 from jax.sharding import PartitionSpec as P
 
-DS, DT, ROWS, EXT = 1024, 4096, 56, 128
+DS, DT, ROWS, LANES = 1024, 4096, 56, 128
 TEXTS = 14336
-WIDTH = DT + DS + EXT
+WIDTH = DT + DS
 PIECES = ((0, 1280), (1280, 2560), (2560, 3840), (3840, WIDTH))
 T_PIECES = ((0, 1280), (1280, 2560), (2560, 3840), (3840, DT))
 LINKS = ("X+", "X-", "Y+", "Y-", "Z+", "Z-", "S")
@@ -234,7 +234,7 @@
     return lax.dot_general(a, b, ((dims[0], dims[1]), ((), ())), preferred_element_type=jnp.float32)
 
 
-def kernel(student, teacher, scales, out, X, acc, D, GI, GJ, RI, RJ, RS, load_sem, send, recv):
+def kernel(student, teacher, scales, out, X, SC, SI, SJ, acc, D, GI, GJ, RI, RJ, RS, load_sem, send, recv):
     row, col = lax.axis_index("row"), lax.axis_index("col")
     z, c = row // 2, row % 2
     x, y = col // 4, col % 4
@@ -255,15 +255,9 @@
     barrier = pltpu.get_barrier_semaphore()
     for link in LINKS:
         pl.semaphore_signal(barrier, inc=1, device_id=peer[link], device_id_type=pl.DeviceIdType.MESH)
-    here = lax.broadcasted_iota(jnp.int32, (ROWS, ROWS), 0) == lax.broadcasted_iota(jnp.int32, (ROWS, ROWS), 1)
-    scale = jnp.sum(jnp.where(here, jnp.broadcast_to(scales[...], (ROWS, ROWS)), 0.0), axis=1, keepdims=True)
-    high = scale.astype(jnp.bfloat16).astype(jnp.float32)
-    mid = (scale - high).astype(jnp.bfloat16).astype(jnp.float32)
-    low = scale - high - mid
-    lane = lax.broadcasted_iota(jnp.int32, (ROWS, EXT), 1)
-    terms = jnp.where(lane == 0, high, jnp.where(lane == 1, mid, jnp.where(lane == 2, low, 0.0)))
-    X[OWN, :, DT + DS:] = terms.astype(jnp.bfloat16)
-    X[OWN_J, :, DT + DS:] = terms.astype(jnp.bfloat16)
+    for own in (OWN, OWN_J):
+        SC[own] = jnp.zeros((8, LANES), jnp.float32)
+        SC[own, 0:1, 0:ROWS] = scales[...]
     for load in loads:
         load.wait()
     pl.semaphore_wait(barrier, len(LINKS))
@@ -284,11 +278,20 @@
         low_col, high_col = PIECES[piece]
         return X.at[index, :, pl.ds(low_col, high_col - low_col)]
 
+    def push_part(link, src, dst, piece):
+        out = [push(link, part(src, piece), part(dst, piece))]
+        if piece == 3:
+            out.append(push(link, SC.at[src], SC.at[dst]))
+        return out
+
     def i_rows(g, a, b):
         return X[4 * g:4 * g + 4, :, a:b].reshape(GROUP, b - a)
 
     def j_rows(g, a, b):
         return X[16 + 4 * g:20 + 4 * g, :, a:b].reshape(GROUP, b - a)
+
+    scaled = set()
+    eye = lax.broadcasted_iota(jnp.int32, (ROWS, ROWS), 0) == lax.broadcasted_iota(jnp.int32, (ROWS, ROWS), 1)
 
     def grad_i(i):
         total = None
@@ -319,40 +322,58 @@
         if kind == "acc":
             acc[i, j, :, :GROUP] = total
             return
-        own = jnp.sum(i_rows(i, DT + DS, WIDTH).astype(jnp.float32), axis=1, keepdims=True)
-        ones = jnp.ones((8, EXT), jnp.bfloat16)
-        other = dot(ones, j_rows(j, DT + DS, WIDTH), ((1,), (1,)))[0:1]
+        if ("i", i) not in scaled:
+            scaled.add(("i", i))
+            for b in range(4 * i, 4 * i + 4):
+                line = jnp.broadcast_to(SC[b, 0:1, 0:ROWS], (ROWS, ROWS))
+                column = jnp.sum(jnp.where(eye, line, 0.0), axis=1, keepdims=True)
+                SI[b] = jnp.broadcast_to(column, (ROWS, LANES))
+        if ("j", j) not in scaled:
+            scaled.add(("j", j))
+            line = jnp.zeros((8, 2 * LANES), jnp.float32)
+            for k in range(4):
+                wide = jnp.concatenate([SC[16 + 4 * j + k], jnp.zeros((8, LANES), jnp.float32)], axis=1)
+                line = line + (pltpu.roll(wide, ROWS * k, 1) if k else wide)
+            SJ[j] = line
+        own = SI[4 * i:4 * i + 4].reshape(GROUP, LANES)[:, 0:1]
+        other = SJ[j, 0:1, 0:GROUP]
         student_gram = dot(i_rows(i, DT, DT + DS), j_rows(j, DT, DT + DS), ((1,), (1,)))
         d = jnp.clip(student_gram - total * own * other, -0.25, 0.25)
         D[i, j, :, :GROUP] = d.astype(jnp.bfloat16)
 
     arriving, forwards = {}, {}
-    first = push("S", X.at[OWN_J], X.at[J_INDEX[(0, 1)]])
+    first = [
+        push("S", X.at[OWN_J], X.at[J_INDEX[(0, 1)]]),
+        push("S", SC.at[OWN_J], SC.at[J_INDEX[(0, 1)]]),
+    ]
 
     def wait_slot(s):
         if s == 0:
-            first.wait_recv()
+            for copy in first:
+                copy.wait_recv()
         for copy in forwards.pop(s - 1, []):
             copy.wait_recv()
         for copy in arriving.pop(("xy", s), []):
             copy.wait_recv()
         for copy, m in arriving.pop(("z", s), []):
             copy.wait_recv()
-            forwards.setdefault(s, []).append(
-                push("S", part(J_INDEX[(m[3], 0)], m[2]), part(J_INDEX[(m[3], 1)], m[2]))
-            )
+            if m is not None:
+                forwards.setdefault(s, []).extend(
+                    push_part("S", J_INDEX[(m[3], 0)], J_INDEX[(m[3], 1)], m[2])
+                )
 
     for now in range(1, LAST + 1):
         if now > LAG - 1:
             wait_slot(now - LAG)
         for i, m in enumerate(MOVES):
             if SLOT[i] == now:
-                copy = push(m[0], part(I_INDEX[m[1]], m[2]), part(I_INDEX[m[3]], m[2]))
-                arriving.setdefault(("xy", now), []).append(copy)
+                arriving.setdefault(("xy", now), []).extend(
+                    push_part(m[0], I_INDEX[m[1]], I_INDEX[m[3]], m[2])
+                )
         for m in Z_MOVES:
             if m[4] == now:
-                copy = push(m[0], part(J_INDEX[(m[1], 0)], m[2]), part(J_INDEX[(m[3], 0)], m[2]))
-                arriving.setdefault(("z", now), []).append((copy, m))
+                pair = push_part(m[0], J_INDEX[(m[1], 0)], J_INDEX[(m[3], 0)], m[2])
+                arriving.setdefault(("z", now), []).extend((copy, m if copy is pair[-1] else None) for copy in pair)
         for task in TASKS[now]:
             run(task)
     for stage in range(LAST - LAG + 1, LAST):
@@ -440,7 +461,7 @@
         copy.wait_send()
 
 
-COPIES = 1 + len(MOVES) + 2 * len(Z_MOVES) + 8 + len(R_MOVES) + len(RZ_MOVES)
+COPIES = 32 + len(MOVES) + 2 * len(Z_MOVES) + 8 + len(R_MOVES) + len(RZ_MOVES)
 
 
 def per_device(student, teacher, scales):
@@ -455,6 +476,9 @@
         out_specs=pl.BlockSpec(memory_space=pltpu.VMEM),
         scratch_shapes=[
             pltpu.VMEM((BLOCKS, ROWS, WIDTH), jnp.bfloat16),
+            pltpu.VMEM((BLOCKS, 8, LANES), jnp.float32),
+            pltpu.VMEM((16, ROWS, LANES), jnp.float32),
+            pltpu.VMEM((4, 8, 2 * LANES), jnp.float32),
             pltpu.VMEM((4, 4, GROUP, 256), jnp.float32),
             pltpu.VMEM((4, 4, GROUP, 256), jnp.bfloat16),
             pltpu.VMEM((4, 16, ROWS, QI), jnp.float32),

time: 87.2 us -> 85.6 us (0.982)
  Pallas kernels: 85.4 us -> 83.8 us
    pallas_call x1, Pallas kernels: 85.4 us -> 83.8 us  [per_device(): pl.pallas_call(kernel, out_shape=jax.ShapeDtypeStruct((ROWS, DS), jnp.flo...]
where the time goes in v3:
time: 85.6 us; the launch traced here: 85.5 us
  Pallas kernels  83.8 us (98%)
  local copies, waits for them, and re-layouts  1.64 us (2%)
    pallas_call x1, Pallas kernels, per_device(): pl.pallas_call(kernel, out_shape=jax.ShapeDtypeStruct((ROWS, DS), jnp.flo...  83.8 us

profile of v3, /device:TPU:6, one launch (start us, length us, event | category | flops | bytes accessed | tf_op | source)
XLA Modules:
  0.0 85.5 jit_solution(10830660629303636287)
XLA Ops:
  0.0 83.8 %huber_gram.1 = f32[56,1024]{1,0:T(8,128)} custom-call(bf16[56,1024]{1,0:T(8,128)(2,1)} %student.1, bf16[56,4096]{1,0:T(8,128)(2,1)} %teacher.1, f32[1,56]{1,0:T(1,128)} %bitcast.1), custom_call_target="tpu_custom_call" | custom-call | flops 10000000000 | bytes 1000000 | tf_op jit(solution)/shard_map/huber_gram/pallas_call | solution.py:468
  83.8 1.6 %copy.5 = f32[56,1024]{1,0:T(8,128)} copy(f32[56,1024]{1,0:T(8,128)} %huber_gram.1) | data formatting | bytes 458752

commit v4 on v3

--- a/solution.py
+++ b/solution.py
@@ -350,13 +350,13 @@
     def wait_slot(s):
         if s == 0:
             for copy in first:
-                copy.wait_recv()
+                copy.wait()
         for copy in forwards.pop(s - 1, []):
-            copy.wait_recv()
+            copy.wait()
         for copy in arriving.pop(("xy", s), []):
-            copy.wait_recv()
+            copy.wait()
         for copy, m in arriving.pop(("z", s), []):
-            copy.wait_recv()
+            copy.wait()
             if m is not None:
                 forwards.setdefault(s, []).extend(
                     push_part("S", J_INDEX[(m[3], 0)], J_INDEX[(m[3], 1)], m[2])
@@ -381,7 +381,7 @@
         for task in TASKS["after", stage]:
             run(task)
     for copy in forwards.pop(LAST - 1, []):
-        copy.wait_recv()
+        copy.wait()
     for task in TASKS["after", LAST]:
         run(task)
     shared, waiting, z_waiting = {}, {}, {}
@@ -397,7 +397,7 @@
     def collect(i):
         if i not in waiting:
             return
-        waiting.pop(i).wait_recv()
+        waiting.pop(i).wait()
         m = R_MOVES[i]
         GI[m[2], I_INDEX[m[3]]] += RI[i]
 
@@ -411,13 +411,13 @@
     def z_collect(i):
         if i not in z_waiting:
             return
-        z_waiting.pop(i).wait_recv()
+        z_waiting.pop(i).wait()
         m = RZ_MOVES[i]
         GJ[m[2], J_INDEX[(m[3], 0)] - 16] += RJ[i]
 
     def join(d):
         if d in shared:
-            shared.pop(d).wait_recv()
+            shared.pop(d).wait()
             GJ[:, J_INDEX[(d, 0)] - 16] += RS[d]
 
     def send_z(i):
@@ -457,8 +457,6 @@
         out[:, q * QI:(q + 1) * QI] = factor * GI[q, I_INDEX[(0, 0)]]
     for h in range(4):
         out[:, WI + h * HJ:WI + (h + 1) * HJ] = factor * GJ[h, 0]
-    for copy in copies:
-        copy.wait_send()
 
 
 COPIES = 32 + len(MOVES) + 2 * len(Z_MOVES) + 8 + len(R_MOVES) + len(RZ_MOVES)

time: 85.6 us -> 85.3 us (level)
  no operation moved by 1% of the time
where the time goes in v4:
time: 85.3 us; the launch traced here: 85.1 us
  Pallas kernels  83.5 us (98%)
  local copies, waits for them, and re-layouts  1.64 us (2%)
    pallas_call x1, Pallas kernels, per_device(): pl.pallas_call(kernel, out_shape=jax.ShapeDtypeStruct((ROWS, DS), jnp.flo...  83.5 us

profile of v4, /device:TPU:6, one launch (start us, length us, event | category | flops | bytes accessed | tf_op | source)
XLA Modules:
  0.0 85.1 jit_solution(15300515825597709985)
XLA Ops:
  0.0 83.5 %huber_gram.1 = f32[56,1024]{1,0:T(8,128)} custom-call(bf16[56,1024]{1,0:T(8,128)(2,1)} %student.1, bf16[56,4096]{1,0:T(8,128)(2,1)} %teacher.1, f32[1,56]{1,0:T(1,128)} %bitcast.1), custom_call_target="tpu_custom_call" | custom-call | flops 10000000000 | bytes 1000000 | tf_op jit(solution)/shard_map/huber_gram/pallas_call | solution.py:466
  83.5 1.6 %copy.5 = f32[56,1024]{1,0:T(8,128)} copy(f32[56,1024]{1,0:T(8,128)} %huber_gram.1) | data formatting | bytes 458752

commit v5 on v4

--- a/solution.py
+++ b/solution.py
@@ -16,7 +16,7 @@
 WI = 512
 WJ = DS - WI
 QI, HJ = WI // 4, WJ // 4
-LAG = 3
+LAG = 2
 BUDGET = 2.2
 HOP = 2.2
 S_HOP = 2.5
@@ -390,9 +390,12 @@
         for task in TASKS["last", j]:
             run(task)
         grad_j(j)
-        for d, core in reversed(J_ORDER[4 * j:4 * j + 4]):
+        for d, core in reversed(J_ORDER[4 * j:4 * j + 4] if j else J_ORDER[2:4]):
             if core == 1:
                 shared[d] = push("S", GJ.at[:, J_INDEX[(d, 1)] - 16], RS.at[d])
+
+    def share(d):
+        shared[d] = push("S", GJ.at[:, J_INDEX[(d, 1)] - 16], RS.at[d])
 
     def collect(i):
         if i not in waiting:
@@ -434,6 +437,7 @@
         clock += 0.3 + 0.75 * len(TASKS["last", j])
         for d, core in J_ORDER[4 * j:4 * j + 4]:
             j_ready[d] = clock + S_HOP
+    steps.append((clock, 9, share, 0))
     for i in TASKS["late"]:
         steps.append((clock, 4 + i, grad_i, i))
         clock += 0.3

time: 85.3 us -> 85.1 us (level)
  no operation moved by 1% of the time
where the time goes in v5:
time: 85.1 us; the launch traced here: 84.9 us
  Pallas kernels  83.3 us (98%)
  local copies, waits for them, and re-layouts  1.64 us (2%)
    pallas_call x1, Pallas kernels, per_device(): pl.pallas_call(kernel, out_shape=jax.ShapeDtypeStruct((ROWS, DS), jnp.flo...  83.3 us

profile of v5, /device:TPU:6, one launch (start us, length us, event | category | flops | bytes accessed | tf_op | source)
XLA Modules:
  0.0 84.9 jit_solution(7000654948393754818)
XLA Ops:
  0.0 83.3 %huber_gram.1 = f32[56,1024]{1,0:T(8,128)} custom-call(bf16[56,1024]{1,0:T(8,128)(2,1)} %student.1, bf16[56,4096]{1,0:T(8,128)(2,1)} %teacher.1, f32[1,56]{1,0:T(1,128)} %bitcast.1), custom_call_target="tpu_custom_call" | custom-call | flops 10000000000 | bytes 1000000 | tf_op jit(solution)/shard_map/huber_gram/pallas_call | solution.py:470
  83.3 1.6 %copy.5 = f32[56,1024]{1,0:T(8,128)} copy(f32[56,1024]{1,0:T(8,128)} %huber_gram.1) | data formatting | bytes 458752

commit v6 on v4

--- a/solution.py
+++ b/solution.py
@@ -18,8 +18,8 @@
 QI, HJ = WI // 4, WJ // 4
 LAG = 3
 BUDGET = 2.2
-HOP = 2.2
-S_HOP = 2.5
+HOP = 1.5
+S_HOP = 1.5
 
 
 def moved(block, link):

time: 85.3 us -> 85.9 us (level)
  no operation moved by 1% of the time
where the time goes in v6:
time: 85.9 us; the launch traced here: 85.8 us
  Pallas kernels  84.1 us (98%)
  local copies, waits for them, and re-layouts  1.64 us (2%)
    pallas_call x1, Pallas kernels, per_device(): pl.pallas_call(kernel, out_shape=jax.ShapeDtypeStruct((ROWS, DS), jnp.flo...  84.1 us

profile of v6, /device:TPU:6, one launch (start us, length us, event | category | flops | bytes accessed | tf_op | source)
XLA Modules:
  0.0 85.8 jit_solution(17411108747775149348)
XLA Ops:
  0.0 84.1 %huber_gram.1 = f32[56,1024]{1,0:T(8,128)} custom-call(bf16[56,1024]{1,0:T(8,128)(2,1)} %student.1, bf16[56,4096]{1,0:T(8,128)(2,1)} %teacher.1, f32[1,56]{1,0:T(1,128)} %bitcast.1), custom_call_target="tpu_custom_call" | custom-call | flops 10000000000 | bytes 1000000 | tf_op jit(solution)/shard_map/huber_gram/pallas_call | solution.py:466
  84.1 1.6 %copy.5 = f32[56,1024]{1,0:T(8,128)} copy(f32[56,1024]{1,0:T(8,128)} %huber_gram.1) | data formatting | bytes 458752
